TPU v7x, 32 devices: a whole 2x2x4 slice. The times are simulated.
32 devices in a mesh: gx: 4 (over y, core), gy: 8 (over z, x).
Axes of the slice: x: 2, y: 2, z: 4, core: 2. Of those that a mesh axis runs over, the one named last changes fastest.
Arguments:
- x_block: float32 [16, 32, 64, 128], P(None, 'gx', 'gy'), may hold values from -8 to 8
- old_direction: float32 [16, 32, 64, 128], P(None, 'gx', 'gy'), may hold values from -6 to 6
- conductivity: float32 [32, 64, 128], P('gx', 'gy'), may hold values from 0.5 to 4
- fsai_diagonal: float32 [32, 64, 128], P('gx', 'gy'), may hold values from 0.2 to 0.6
- fsai_lower: float32 [13, 32, 64, 128], P(None, 'gx', 'gy'), may hold values from -0.9 to 0.9
- pattern: int32 [8, 13], replicated, may hold values 0 or 1
- step_size: float32 [16], replicated, may hold values from 0.3 to 1.5
- momentum: float32 [16], replicated, may hold values from 0.2 to 1
Outputs:
- x_next: float32 [16, 32, 64, 128], P(None, 'gx', 'gy')
- direction: float32 [16, 32, 64, 128], P(None, 'gx', 'gy')
- rayleigh: float32 [16, 16], replicated
All inputs are finite; a program needn't handle non-finite values.
Results may differ from a plain program's by a relative error of at most 0.00018.
Values sent between devices are 32-bit elements; how exact they have to be, the bound alone decides.
A program may use at most 64 MiB of HBM per device.

v0:
```python
import jax
import jax.numpy as jnp
from jax import lax
from jax.sharding import PartitionSpec as P

BLOCKS = 8
lower_offsets = [
    (a, b, c) for a in (-1, 0, 1) for b in (-1, 0, 1) for c in (-1, 0, 1) if (a, b, c) < (0, 0, 0)
]
face_offsets = [(1, 0, 0), (-1, 0, 0), (0, 1, 0), (0, -1, 0), (0, 0, 1), (0, 0, -1)]


def extended(cells, sides, width):
    for axis, dim in sides:
        count = lax.axis_size(axis)
        ends = count - 1
        head = lax.slice_in_dim(cells, 0, width, axis=dim)
        tail = lax.slice_in_dim(cells, cells.shape[dim] - width, cells.shape[dim], axis=dim)
        cells = jnp.concatenate(
            [
                lax.ppermute(tail, axis, [(i, (i + 1) % count) for i in range(ends)]),
                cells,
                lax.ppermute(head, axis, [((i + 1) % count, i) for i in range(ends)]),
            ],
            axis=dim,
        )
    return cells


def passed_along(array, axis, by):
    size = lax.axis_size(axis)
    pairs = [(i, i + by) for i in range(size) if 0 <= i + by < size]
    return lax.ppermute(array, axis, pairs)


def window(padded, step_x, step_y, step_z, region):
    size_x, size_y, size_z = region
    return padded[
        ...,
        1 + step_x : 1 + step_x + size_x,
        1 + step_y : 1 + step_y + size_y,
        1 + step_z : 1 + step_z + size_z,
    ]


def apply_stiffness(padded, kappa_pad, region):
    centre = window(padded, 0, 0, 0, region)
    kappa_here = window(kappa_pad, 0, 0, 0, region)
    summed = jnp.zeros(centre.shape, jnp.float32)
    for step_x, step_y, step_z in face_offsets:
        face = 0.5 * (kappa_here + window(kappa_pad, step_x, step_y, step_z, region))
        summed = summed + face * (centre - window(padded, step_x, step_y, step_z, region))
    return summed


def apply_factor(padded, diag_here, lower_here, region):
    summed = diag_here * window(padded, 0, 0, 0, region)
    for index, (step_x, step_y, step_z) in enumerate(lower_offsets):
        summed = summed + lower_here[index] * window(padded, step_x, step_y, step_z, region)
    return summed


def apply_transpose(padded, diag_pad, lower_pad, region):
    summed = window(diag_pad, 0, 0, 0, region) * window(padded, 0, 0, 0, region)
    for index, (step_x, step_y, step_z) in enumerate(lower_offsets):
        summed = summed + window(lower_pad[index], -step_x, -step_y, -step_z, region) * window(
            padded, -step_x, -step_y, -step_z, region
        )
    return summed


def pad_depth(field):
    widths = [(0, 0)] * (field.ndim - 1) + [(1, 1)]
    return jnp.pad(field, widths)


def quotient_of(x_block, image, scale):
    local_xx = jnp.sum(x_block * x_block, axis=(1, 2, 3))
    local_xa = jnp.sum(x_block * image, axis=(1, 2, 3))
    sum_xx, sum_xa = lax.psum((local_xx, local_xa), ("gx", "gy"))
    return sum_xa * scale / (sum_xx * scale + 1e-06)


def per_device(
    x_block, old_direction, conductivity, fsai_diagonal, fsai_lower, pattern, step_size, momentum
):
    size_x = x_block.shape[1]
    size_y = x_block.shape[2]
    size_z = x_block.shape[3]
    region = (size_x, size_y, size_z)
    vectors = x_block.shape[0]
    cell_count = size_x * size_y * size_z * lax.axis_size("gx") * lax.axis_size("gy")
    scale = 1.0 / cell_count
    block_id = jnp.arange(size_z, dtype=jnp.int32) // (size_z // BLOCKS)
    onehot = (block_id[:, None] == jnp.arange(BLOCKS, dtype=jnp.int32)[None, :]).astype(jnp.float32)
    active = jnp.dot(onehot, pattern.astype(jnp.float32), precision=lax.Precision.HIGHEST)
    lower_terms = fsai_lower * jnp.transpose(active)[:, None, None, :]
    fields = jnp.concatenate([conductivity[None], fsai_diagonal[None], lower_terms], axis=0)
    fields_wide = extended(fields, (("gx", 1), ("gy", 2)), 1)
    block_wide = pad_depth(extended(x_block, (("gx", 1), ("gy", 2)), 1))
    fields_pad = pad_depth(fields_wide)
    kappa_pad = fields_pad[0]
    diag_pad = fields_pad[1]
    lower_pad = fields_pad[2:]
    image = apply_stiffness(block_wide, kappa_pad, region)
    quotient = quotient_of(x_block, image, scale)
    gradient = image - quotient[:, None, None, None] * x_block
    near_pad = pad_depth(extended(gradient, (("gx", 1), ("gy", 2)), 1))
    product = apply_factor(near_pad, fsai_diagonal, lower_terms, region)
    side_wide = extended(product, (("gy", 2),), 1)
    upper_plane = passed_along(side_wide[:, :1], "gx", -1)
    lower_plane = jnp.zeros(upper_plane.shape, jnp.float32)
    product_pad = pad_depth(jnp.concatenate([lower_plane, side_wide, upper_plane], axis=1))
    smoothed = apply_transpose(product_pad, diag_pad, lower_pad, region)
    direction = smoothed + momentum[:, None, None, None] * old_direction
    direction_pad = pad_depth(extended(direction, (("gx", 1), ("gy", 2)), 1))
    direction_image = apply_stiffness(direction_pad, kappa_pad, region)
    advanced = x_block + step_size[:, None, None, None] * direction
    advanced_image = image + step_size[:, None, None, None] * direction_image
    local_gram = jnp.einsum("kxyz,jxyz->kj", advanced, advanced, precision=lax.Precision.HIGHEST)
    local_stiff = jnp.einsum(
        "kxyz,jxyz->kj", advanced, advanced_image, precision=lax.Precision.HIGHEST
    )
    gram_total, stiff_total = lax.psum((local_gram, local_stiff), ("gx", "gy"))
    identity = jnp.eye(vectors, dtype=jnp.float32)
    gram = gram_total * scale + 1e-05 * identity
    stiff = stiff_total * scale
    factor = jnp.linalg.cholesky(gram)
    inverse = jax.scipy.linalg.solve_triangular(factor, identity, lower=True)
    x_next = jnp.einsum("kj,jxyz->kxyz", inverse, advanced, precision=lax.Precision.HIGHEST)
    rayleigh = jnp.dot(
        jnp.dot(inverse, stiff, precision=lax.Precision.HIGHEST),
        jnp.transpose(inverse),
        precision=lax.Precision.HIGHEST,
    )
    return (x_next, direction, rayleigh)


def solution(mesh):
    placed = (
        P(None, "gx", "gy", None),
        P(None, "gx", "gy", None),
        P("gx", "gy", None),
        P("gx", "gy", None),
        P(None, "gx", "gy", None),
        P(),
        P(),
        P(),
    )
    return jax.shard_map(
        per_device,
        mesh=mesh,
        in_specs=placed,
        out_specs=(P(None, "gx", "gy", None), P(None, "gx", "gy", None), P()),
        check_vma=False,
    )
```

profile of v0, /device:TPU:0, one launch (start us, length us, event | category | flops | bytes accessed | tf_op | source)
XLA Modules:
  0.0 178.6 jit_solution(10476219828083600883)
XLA Ops:
  0.6 0.9 convolution_bitcast_fusion.2
  1.6 1.1 broadcast_multiply_fusion
  2.7 0.7 pad_maximum_fusion.38
  3.5 2.4 %collective-permute-start = (f32[15,1,8,128]{3,2,1,0:T(8,128)S(1)}, f32[15,1,8,128]{3,2,1,0:T(8,128)S(1)}, u32[]{:S(2)}, u32[]{:S(2)}) collective-permute-start(f32[15,1,8,128]{3,2,1,0:T(8,128)S(1)} %get-tuple-element.49), channel_id=1, source_target_pairs={{0,8},{8,16},{16,24},{1,9},{9,17},{17,25},{2,10},{10,18},{18,26},{... | collective-permute-start | bytes 184328 | tf_op jit(solution)/shard_map/ppermute | solution.py:21
  5.8 1.3 collective-permute-start.1
  7.5 5.2 %collective-permute-start.5 = (f32[16,1,8,128]{3,0,2,1:T(8,128)S(1)}, f32[16,1,8,128]{3,0,2,1:T(8,128)S(1)}, u32[]{:S(2)}, u32[]{:S(2)}) collective-permute-start(f32[16,1,8,128]{3,0,2,1:T(8,128)S(1)} %get-tuple-element.48), channel_id=1, source_target_pairs={{0,8},{8,16},{16,24},{1,9},{9,17},{17,25},{2,10},{10,18},{18,26},{... | collective-permute-start | bytes 196616 | tf_op jit(solution)/shard_map/ppermute | solution.py:21
  12.6 1.3 collective-permute-start.4
  14.3 3.4 %collective-permute-start.2 = (f32[15,10,1,128]{3,0,2,1:T(8,128)S(1)}, f32[15,10,1,128]{3,0,2,1:T(8,128)S(1)}, u32[]{:S(2)}, u32[]{:S(2)}) collective-permute-start(f32[15,10,1,128]{3,0,2,1:T(8,128)S(1)} %copy.35), channel_id=1, source_target_pairs={{0,1},{1,2},{2,3},{3,4},{4,5},{5,6},{6,7},{8,9},{9,10},{10,11},{11... | collective-permute-start | bytes 230408 | tf_op jit(solution)/shard_map/ppermute | solution.py:21
  17.7 1.3 collective-permute-start.3
  19.4 1.3 collective-permute-start.6
  20.7 5.2 %collective-permute-start.7 = (f32[16,10,1,128]{3,0,2,1:T(8,128)S(1)}, f32[16,10,1,128]{3,0,2,1:T(8,128)S(1)}, u32[]{:S(2)}, u32[]{:S(2)}) collective-permute-start(f32[16,10,1,128]{3,0,2,1:T(8,128)S(1)} %get-tuple-element.37), channel_id=1, source_target_pairs={{0,1},{1,2},{2,3},{3,4},{4,5},{5,6},{6,7},{8,9},{9,10},{10,11},{11... | collective-permute-start | bytes 245768 | tf_op jit(solution)/shard_map/ppermute | solution.py:21
  26.1 2.8 %select_maximum_fusion = f32[15,10,10,130]{3,2,1,0:T(8,128)S(1)} fusion(f32[15,10,1,128]{3,2,1,0:T(1,128)S(1)} %copy.38, f32[15,10,1,128]{3,2,1,0:T(1,128)S(1)} %copy.37, f32[15,1,8,128]{3,2,1,0:T(8,128)S(1)} %collective-permute-done.1, f32[15,1,8,128]{3,2,1,0:T(8,128)S(1)} %collective-permute-done, f32[13,8,8,128]{3,2,1,0:T(8,128)S(1)} %broadcast_multiply_fusion, ...), kind=kLoop, calls=%fused_computation.13 | loop fusion | flops 3120000 | bytes 1548000 | tf_op jit(solution)/shard_map/concatenate | solution.py:19
  28.9 1.0 slice_bitcast_fusion.14
  30.6 0.8 multiply_reduce_fusion.1
  31.4 44.4 %all-reduce.6 = (f32[16]{0:T(128)S(1)}, f32[16]{0:T(128)S(1)}) all-reduce(f32[16]{0:T(128)S(1)} %multiply_reduce_fusion, f32[16]{0:T(128)S(1)} %get-tuple-element.16), channel_id=1, replica_groups=mesh['gx'=4,'gy'=8] {'gx','gy'}, use_global_device_ids=true, to_apply=%region_3.4 | all-reduce | flops 32 | bytes 256 | tf_op jit(solution)/shard_map/psum | solution.py:80
  76.2 1.3 collective-permute-start.8
  77.5 1.3 collective-permute-start.9
  78.8 4.3 %collective-permute-done.9 = f32[16,1,8,128]{3,0,2,1:T(8,128)S(1)} collective-permute-done((f32[16,1,8,128]{3,0,2,1:T(8,128)S(1)}, f32[16,1,8,128]{3,0,2,1:T(8,128)S(1)}, u32[]{:S(2)}, u32[]{:S(2)}) %collective-permute-start.9) | collective-permute-done | bytes 65568 | tf_op jit(solution)/shard_map/ppermute | solution.py:23
  83.1 2.5 %collective-permute-start.10 = (f32[16,10,1,128]{3,0,2,1:T(8,128)S(1)}, f32[16,10,1,128]{3,0,2,1:T(8,128)S(1)}, u32[]{:S(2)}, u32[]{:S(2)}) collective-permute-start(f32[16,10,1,128]{3,0,2,1:T(8,128)S(1)} %get-tuple-element.35), channel_id=1, source_target_pairs={{0,1},{1,2},{2,3},{3,4},{4,5},{5,6},{6,7},{8,9},{9,10},{10,11},{11... | collective-permute-start | bytes 245768 | tf_op jit(solution)/shard_map/ppermute | solution.py:21
  85.7 1.3 collective-permute-start.11
  87.0 0.7 collective-permute-done.10
  87.8 4.3 %collective-permute-done.11 = f32[16,10,1,128]{3,0,2,1:T(8,128)S(1)} collective-permute-done((f32[16,10,1,128]{3,0,2,1:T(8,128)S(1)}, f32[16,10,1,128]{3,0,2,1:T(8,128)S(1)}, u32[]{:S(2)}, u32[]{:S(2)}) %collective-permute-start.11) | collective-permute-done | bytes 81952 | tf_op jit(solution)/shard_map/ppermute | solution.py:23
  92.5 0.8 fusion.53
  93.4 3.9 %collective-permute-start.12 = (f32[16,8,1,128]{3,0,2,1:T(8,128)S(1)}, f32[16,8,1,128]{3,0,2,1:T(8,128)S(1)}, u32[]{:S(2)}, u32[]{:S(2)}) collective-permute-start(f32[16,8,1,128]{3,0,2,1:T(8,128)S(1)} %get-tuple-element.43), channel_id=1, source_target_pairs={{0,1},{1,2},{2,3},{3,4},{4,5},{5,6},{6,7},{8,9},{9,10},{10,11},{11... | collective-permute-start | bytes 196616 | tf_op jit(solution)/shard_map/ppermute | solution.py:21
  97.3 1.3 collective-permute-start.13
  98.6 0.7 collective-permute-done.12
  99.3 4.6 %collective-permute-done.13 = f32[16,8,1,128]{3,0,2,1:T(8,128)S(1)} collective-permute-done((f32[16,8,1,128]{3,0,2,1:T(8,128)S(1)}, f32[16,8,1,128]{3,0,2,1:T(8,128)S(1)}, u32[]{:S(2)}, u32[]{:S(2)}) %collective-permute-start.13) | collective-permute-done | bytes 65568 | tf_op jit(solution)/shard_map/ppermute | solution.py:23
  103.9 1.3 collective-permute-start.14
  105.2 1.0 slice.508
  106.2 1.0 slice.550
  108.1 0.6 copy-done.2
  108.7 1.3 fusion.16
  110.0 1.3 collective-permute-start.15
  111.3 4.5 %collective-permute-start.16 = (f32[16,1,8,128]{3,0,2,1:T(8,128)S(1)}, f32[16,1,8,128]{3,0,2,1:T(8,128)S(1)}, u32[]{:S(2)}, u32[]{:S(2)}) collective-permute-start(f32[16,1,8,128]{3,0,2,1:T(8,128)S(1)} %get-tuple-element.41), channel_id=1, source_target_pairs={{0,8},{8,16},{16,24},{1,9},{9,17},{17,25},{2,10},{10,18},{18,26},{... | collective-permute-start | bytes 196616 | tf_op jit(solution)/shard_map/ppermute | solution.py:21
  115.8 1.0 copy.56
  116.8 1.3 collective-permute-start.17
  118.1 4.9 %collective-permute-start.18 = (f32[16,10,1,128]{3,0,2,1:T(8,128)S(1)}, f32[16,10,1,128]{3,0,2,1:T(8,128)S(1)}, u32[]{:S(2)}, u32[]{:S(2)}) collective-permute-start(f32[16,10,1,128]{3,0,2,1:T(8,128)S(1)} %get-tuple-element.33), channel_id=1, source_target_pairs={{0,1},{1,2},{2,3},{3,4},{4,5},{5,6},{6,7},{8,9},{9,10},{10,11},{11... | collective-permute-start | bytes 245768 | tf_op jit(solution)/shard_map/ppermute | solution.py:21
  123.0 1.0 convolution_bitcast_fusion.1
  124.0 1.9 %collective-permute-done.18 = f32[16,10,1,128]{3,0,2,1:T(8,128)S(1)} collective-permute-done((f32[16,10,1,128]{3,0,2,1:T(8,128)S(1)}, f32[16,10,1,128]{3,0,2,1:T(8,128)S(1)}, u32[]{:S(2)}, u32[]{:S(2)}) %collective-permute-start.18) | collective-permute-done | bytes 81952 | tf_op jit(solution)/shard_map/ppermute | solution.py:21
  126.5 1.4 convolution_bitcast_fusion
  127.8 43.8 %all-reduce.5 = (f32[16,16]{1,0:T(8,128)S(1)}, f32[16,16]{1,0:T(8,128)S(1)}) all-reduce(f32[16,16]{1,0:T(8,128)S(1)} %convolution_bitcast_fusion.1, f32[16,16]{1,0:T(8,128)S(1)} %convolution_bitcast_fusion), channel_id=1, replica_groups=mesh['gx'=4,'gy'=8] {'gx','gy'}, use_global_device_ids=true, to_apply=%region_4.5 | all-reduce | flops 512 | bytes 4096 | tf_op jit(solution)/shard_map/psum | solution.py:124
  171.7 1.5 cholesky.17
  173.2 0.6 compare_reduce_fusion
  173.8 0.6 fusion.97
  174.5 1.2 custom-call.7
  175.9 0.9 fusion.98
  176.9 0.7 fusion.118
  177.6 1.0 copy.55
  (96 shorter events, 4.6 us)
Async XLA Ops:
  0.6 6.5 %copy-start = (f32[16,8,8,128]{3,2,1,0:T(8,128)S(1)}, f32[16,8,8,128]{3,2,1,0:T(8,128)}, u32[]{:S(2)}) copy-start(f32[16,8,8,128]{3,2,1,0:T(8,128)} %param.8) | copy-start | bytes 1572868
  1.6 12.6 %copy-start.1 = (f32[8,8,128]{2,1,0:T(8,128)S(1)}, f32[8,8,128]{2,1,0:T(8,128)}, u32[]{:S(2)}) copy-start(f32[8,8,128]{2,1,0:T(8,128)} %param.11) | copy-start | bytes 98308
  1.6 12.6 %copy-start.3 = (f32[8,8,128]{2,1,0:T(8,128)S(1)}, f32[8,8,128]{2,1,0:T(8,128)}, u32[]{:S(2)}) copy-start(f32[8,8,128]{2,1,0:T(8,128)} %param.10) | copy-start | bytes 98308
  3.5 10.7 %collective-permute-start = (f32[15,1,8,128]{3,2,1,0:T(8,128)S(1)}, f32[15,1,8,128]{3,2,1,0:T(8,128)S(1)}, u32[]{:S(2)}, u32[]{:S(2)}) collective-permute-start(f32[15,1,8,128]{3,2,1,0:T(8,128)S(1)} %get-tuple-element.49), channel_id=1, source_target_pairs={{0,8},{8,16},{16,24},{1,9},{9,17},{17,25},{2,10},{10,18},{18,26},{... | collective-permute-start | bytes 184328 | tf_op jit(solution)/shard_map/ppermute | solution.py:21
  5.8 8.3 %collective-permute-start.1 = (f32[15,1,8,128]{3,2,1,0:T(8,128)S(1)}, f32[15,1,8,128]{3,2,1,0:T(8,128)S(1)}, u32[]{:S(2)}, u32[]{:S(2)}) collective-permute-start(f32[15,1,8,128]{3,2,1,0:T(8,128)S(1)} %get-tuple-element.50), channel_id=1, source_target_pairs={{8,0},{16,8},{24,16},{9,1},{17,9},{25,17},{10,2},{18,10},{26,18},{... | collective-permute-start | bytes 184328 | tf_op jit(solution)/shard_map/ppermute | solution.py:23
  7.5 11.6 %collective-permute-start.5 = (f32[16,1,8,128]{3,0,2,1:T(8,128)S(1)}, f32[16,1,8,128]{3,0,2,1:T(8,128)S(1)}, u32[]{:S(2)}, u32[]{:S(2)}) collective-permute-start(f32[16,1,8,128]{3,0,2,1:T(8,128)S(1)} %get-tuple-element.48), channel_id=1, source_target_pairs={{0,8},{8,16},{16,24},{1,9},{9,17},{17,25},{2,10},{10,18},{18,26},{... | collective-permute-start | bytes 196616 | tf_op jit(solution)/shard_map/ppermute | solution.py:21
  12.6 6.7 %collective-permute-start.4 = (f32[16,1,8,128]{3,0,2,1:T(8,128)S(1)}, f32[16,1,8,128]{3,0,2,1:T(8,128)S(1)}, u32[]{:S(2)}, u32[]{:S(2)}) collective-permute-start(f32[16,1,8,128]{3,0,2,1:T(8,128)S(1)} %get-tuple-element.47), channel_id=1, source_target_pairs={{8,0},{16,8},{24,16},{9,1},{17,9},{25,17},{10,2},{18,10},{26,18},{... | collective-permute-start | bytes 196616 | tf_op jit(solution)/shard_map/ppermute | solution.py:23
  14.3 11.6 %collective-permute-start.2 = (f32[15,10,1,128]{3,0,2,1:T(8,128)S(1)}, f32[15,10,1,128]{3,0,2,1:T(8,128)S(1)}, u32[]{:S(2)}, u32[]{:S(2)}) collective-permute-start(f32[15,10,1,128]{3,0,2,1:T(8,128)S(1)} %copy.35), channel_id=1, source_target_pairs={{0,1},{1,2},{2,3},{3,4},{4,5},{5,6},{6,7},{8,9},{9,10},{10,11},{11... | collective-permute-start | bytes 230408 | tf_op jit(solution)/shard_map/ppermute | solution.py:21
  17.7 8.3 %collective-permute-start.3 = (f32[15,10,1,128]{3,0,2,1:T(8,128)S(1)}, f32[15,10,1,128]{3,0,2,1:T(8,128)S(1)}, u32[]{:S(2)}, u32[]{:S(2)}) collective-permute-start(f32[15,10,1,128]{3,0,2,1:T(8,128)S(1)} %copy.36), channel_id=1, source_target_pairs={{1,0},{2,1},{3,2},{4,3},{5,4},{6,5},{7,6},{9,8},{10,9},{11,10},{12... | collective-permute-start | bytes 230408 | tf_op jit(solution)/shard_map/ppermute | solution.py:23
  19.4 10.7 %collective-permute-start.6 = (f32[16,10,1,128]{3,0,2,1:T(8,128)S(1)}, f32[16,10,1,128]{3,0,2,1:T(8,128)S(1)}, u32[]{:S(2)}, u32[]{:S(2)}) collective-permute-start(f32[16,10,1,128]{3,0,2,1:T(8,128)S(1)} %get-tuple-element.38), channel_id=1, source_target_pairs={{1,0},{2,1},{3,2},{4,3},{5,4},{6,5},{7,6},{9,8},{10,9},{11,10},{12... | collective-permute-start | bytes 245768 | tf_op jit(solution)/shard_map/ppermute | solution.py:23
  20.7 9.4 %collective-permute-start.7 = (f32[16,10,1,128]{3,0,2,1:T(8,128)S(1)}, f32[16,10,1,128]{3,0,2,1:T(8,128)S(1)}, u32[]{:S(2)}, u32[]{:S(2)}) collective-permute-start(f32[16,10,1,128]{3,0,2,1:T(8,128)S(1)} %get-tuple-element.37), channel_id=1, source_target_pairs={{0,1},{1,2},{2,3},{3,4},{4,5},{5,6},{6,7},{8,9},{9,10},{10,11},{11... | collective-permute-start | bytes 245768 | tf_op jit(solution)/shard_map/ppermute | solution.py:21
  30.0 1.4 copy-start.4
  30.0 1.3 copy-start.6
  30.1 1.3 copy-start.8
  30.1 1.3 copy-start.10
  30.1 1.3 copy-start.12
  30.1 1.3 copy-start.14
  76.2 2.6 %collective-permute-start.8 = (f32[16,1,8,128]{3,0,2,1:T(8,128)S(1)}, f32[16,1,8,128]{3,0,2,1:T(8,128)S(1)}, u32[]{:S(2)}, u32[]{:S(2)}) collective-permute-start(f32[16,1,8,128]{3,0,2,1:T(8,128)S(1)} %get-tuple-element.45), channel_id=1, source_target_pairs={{0,8},{8,16},{16,24},{1,9},{9,17},{17,25},{2,10},{10,18},{18,26},{... | collective-permute-start | bytes 196616 | tf_op jit(solution)/shard_map/ppermute | solution.py:21
  77.5 5.7 %collective-permute-start.9 = (f32[16,1,8,128]{3,0,2,1:T(8,128)S(1)}, f32[16,1,8,128]{3,0,2,1:T(8,128)S(1)}, u32[]{:S(2)}, u32[]{:S(2)}) collective-permute-start(f32[16,1,8,128]{3,0,2,1:T(8,128)S(1)} %get-tuple-element.46), channel_id=1, source_target_pairs={{8,0},{16,8},{24,16},{9,1},{17,9},{25,17},{10,2},{18,10},{26,18},{... | collective-permute-start | bytes 196616 | tf_op jit(solution)/shard_map/ppermute | solution.py:23
  83.1 4.6 %collective-permute-start.10 = (f32[16,10,1,128]{3,0,2,1:T(8,128)S(1)}, f32[16,10,1,128]{3,0,2,1:T(8,128)S(1)}, u32[]{:S(2)}, u32[]{:S(2)}) collective-permute-start(f32[16,10,1,128]{3,0,2,1:T(8,128)S(1)} %get-tuple-element.35), channel_id=1, source_target_pairs={{0,1},{1,2},{2,3},{3,4},{4,5},{5,6},{6,7},{8,9},{9,10},{10,11},{11... | collective-permute-start | bytes 245768 | tf_op jit(solution)/shard_map/ppermute | solution.py:21
  85.7 6.3 %collective-permute-start.11 = (f32[16,10,1,128]{3,0,2,1:T(8,128)S(1)}, f32[16,10,1,128]{3,0,2,1:T(8,128)S(1)}, u32[]{:S(2)}, u32[]{:S(2)}) collective-permute-start(f32[16,10,1,128]{3,0,2,1:T(8,128)S(1)} %get-tuple-element.36), channel_id=1, source_target_pairs={{1,0},{2,1},{3,2},{4,3},{5,4},{6,5},{7,6},{9,8},{10,9},{11,10},{12... | collective-permute-start | bytes 245768 | tf_op jit(solution)/shard_map/ppermute | solution.py:23
  93.4 5.9 %collective-permute-start.12 = (f32[16,8,1,128]{3,0,2,1:T(8,128)S(1)}, f32[16,8,1,128]{3,0,2,1:T(8,128)S(1)}, u32[]{:S(2)}, u32[]{:S(2)}) collective-permute-start(f32[16,8,1,128]{3,0,2,1:T(8,128)S(1)} %get-tuple-element.43), channel_id=1, source_target_pairs={{0,1},{1,2},{2,3},{3,4},{4,5},{5,6},{6,7},{8,9},{9,10},{10,11},{11... | collective-permute-start | bytes 196616 | tf_op jit(solution)/shard_map/ppermute | solution.py:21
  97.3 6.6 %collective-permute-start.13 = (f32[16,8,1,128]{3,0,2,1:T(8,128)S(1)}, f32[16,8,1,128]{3,0,2,1:T(8,128)S(1)}, u32[]{:S(2)}, u32[]{:S(2)}) collective-permute-start(f32[16,8,1,128]{3,0,2,1:T(8,128)S(1)} %get-tuple-element.44), channel_id=1, source_target_pairs={{1,0},{2,1},{3,2},{4,3},{5,4},{6,5},{7,6},{9,8},{10,9},{11,10},{12... | collective-permute-start | bytes 196616 | tf_op jit(solution)/shard_map/ppermute | solution.py:23
  103.9 4.0 %collective-permute-start.14 = (f32[16,1,10,128]{3,0,2,1:T(8,128)S(1)}, f32[16,1,10,128]{3,0,2,1:T(8,128)S(1)}, u32[]{:S(2)}, u32[]{:S(2)}) collective-permute-start(f32[16,1,10,128]{3,0,2,1:T(8,128)S(1)} %pad_maximum_fusion.26), channel_id=1, source_target_pairs={{8,0},{16,8},{24,16},{9,1},{17,9},{25,17},{10,2},{18,10},{26,18},{... | collective-permute-start | bytes 245768 | tf_op jit(solution)/shard_map/ppermute | solution.py:33
  107.6 1.0 copy-start.2
  107.6 1.0 copy-start.17
  110.0 13.0 %copy-start.16 = (f32[16]{0:T(128)S(1)}, f32[16]{0:T(128)}, u32[]{:S(2)}) copy-start(f32[16]{0:T(128)} %param.14) | copy-start | bytes 196
  110.0 6.7 %collective-permute-start.15 = (f32[16,1,8,128]{3,0,2,1:T(8,128)S(1)}, f32[16,1,8,128]{3,0,2,1:T(8,128)S(1)}, u32[]{:S(2)}, u32[]{:S(2)}) collective-permute-start(f32[16,1,8,128]{3,0,2,1:T(8,128)S(1)} %get-tuple-element.42), channel_id=1, source_target_pairs={{8,0},{16,8},{24,16},{9,1},{17,9},{25,17},{10,2},{18,10},{26,18},{... | collective-permute-start | bytes 196616 | tf_op jit(solution)/shard_map/ppermute | solution.py:23
  111.3 5.4 %collective-permute-start.16 = (f32[16,1,8,128]{3,0,2,1:T(8,128)S(1)}, f32[16,1,8,128]{3,0,2,1:T(8,128)S(1)}, u32[]{:S(2)}, u32[]{:S(2)}) collective-permute-start(f32[16,1,8,128]{3,0,2,1:T(8,128)S(1)} %get-tuple-element.41), channel_id=1, source_target_pairs={{0,8},{8,16},{16,24},{1,9},{9,17},{17,25},{2,10},{10,18},{18,26},{... | collective-permute-start | bytes 196616 | tf_op jit(solution)/shard_map/ppermute | solution.py:21
  116.8 7.2 %collective-permute-start.17 = (f32[16,10,1,128]{3,0,2,1:T(8,128)S(1)}, f32[16,10,1,128]{3,0,2,1:T(8,128)S(1)}, u32[]{:S(2)}, u32[]{:S(2)}) collective-permute-start(f32[16,10,1,128]{3,0,2,1:T(8,128)S(1)} %get-tuple-element.34), channel_id=1, source_target_pairs={{1,0},{2,1},{3,2},{4,3},{5,4},{6,5},{7,6},{9,8},{10,9},{11,10},{12... | collective-permute-start | bytes 245768 | tf_op jit(solution)/shard_map/ppermute | solution.py:23
  118.1 8.3 %copy-start.5 = (f32[8,8,128]{2,1,0:T(8,128)S(1)}, f32[8,8,128]{2,1,0:T(8,128)}, u32[]{:S(2)}) copy-start(f32[8,8,128]{2,1,0:T(8,128)} %copy-done.4) | copy-start | bytes 98308
  118.1 8.3 %copy-start.7 = (f32[8,8,128]{2,1,0:T(8,128)S(1)}, f32[8,8,128]{2,1,0:T(8,128)}, u32[]{:S(2)}) copy-start(f32[8,8,128]{2,1,0:T(8,128)} %copy-done.6) | copy-start | bytes 98308
  118.1 8.3 %copy-start.9 = (f32[8,8,128]{2,1,0:T(8,128)S(1)}, f32[8,8,128]{2,1,0:T(8,128)}, u32[]{:S(2)}) copy-start(f32[8,8,128]{2,1,0:T(8,128)} %copy-done.8) | copy-start | bytes 98308
  118.1 8.3 %copy-start.11 = (f32[8,8,128]{2,1,0:T(8,128)S(1)}, f32[8,8,128]{2,1,0:T(8,128)}, u32[]{:S(2)}) copy-start(f32[8,8,128]{2,1,0:T(8,128)} %copy-done.10) | copy-start | bytes 98308
  118.1 8.3 %copy-start.13 = (f32[8,8,128]{2,1,0:T(8,128)S(1)}, f32[8,8,128]{2,1,0:T(8,128)}, u32[]{:S(2)}) copy-start(f32[8,8,128]{2,1,0:T(8,128)} %copy-done.12) | copy-start | bytes 98308
  118.1 8.3 %copy-start.15 = (f32[8,8,128]{2,1,0:T(8,128)S(1)}, f32[8,8,128]{2,1,0:T(8,128)}, u32[]{:S(2)}) copy-start(f32[8,8,128]{2,1,0:T(8,128)} %copy-done.14) | copy-start | bytes 98308
  118.1 7.8 %collective-permute-start.18 = (f32[16,10,1,128]{3,0,2,1:T(8,128)S(1)}, f32[16,10,1,128]{3,0,2,1:T(8,128)S(1)}, u32[]{:S(2)}, u32[]{:S(2)}) collective-permute-start(f32[16,10,1,128]{3,0,2,1:T(8,128)S(1)} %get-tuple-element.33), channel_id=1, source_target_pairs={{0,1},{1,2},{2,3},{3,4},{4,5},{5,6},{6,7},{8,9},{9,10},{10,11},{11... | collective-permute-start | bytes 245768 | tf_op jit(solution)/shard_map/ppermute | solution.py:21
where the time goes:
time: 180 us; the launch traced here: 179 us
  blocking collectives  88.1 us (49%)
  starting transfers between devices  46.1 us (26%)
  waiting for transfers between devices  16.5 us (9%)
  other arithmetic  14 us (8%)
  local copies, waits for them, and re-layouts  7.16 us (4%)
  matrix products  5.21 us (3%)
    psum x1, blocking collectives, quotient_of(): sum_xx, sum_xa = lax.psum((local_xx, local_xa), ('gx', 'gy'))  44.4 us
    psum x1, blocking collectives, per_device(): gram_total, stiff_total = lax.psum((local_gram, local_stiff), ('gx', 'gy'))  43.8 us
    ppermute x9, starting transfers between devices, extended(): lax.ppermute(tail, axis, [(i, (i + 1) % count) for i in range(ends)])  33.2 us
    ppermute x9, waiting for transfers between devices, extended(): lax.ppermute(head, axis, [((i + 1) % count, i) for i in range(ends)])  13.2 us
    ppermute x9, starting transfers between devices, extended(): lax.ppermute(head, axis, [((i + 1) % count, i) for i in range(ends)])  11.6 us
    concatenate x7, other arithmetic, extended(): jnp.concatenate([lax.ppermute(tail, axis, [(i, (i + 1) % count) for i in...  4.35 us
  transfers between devices with their start and end apart: 19, of which 6 were waited for; matrix products, arithmetic and copies ran while one was open for 5% of the time, Pallas kernels for 0%

commit v1 on v0

--- a/solution.py
+++ b/solution.py
@@ -77,7 +77,11 @@
 def quotient_of(x_block, image, scale):
     local_xx = jnp.sum(x_block * x_block, axis=(1, 2, 3))
     local_xa = jnp.sum(x_block * image, axis=(1, 2, 3))
-    sum_xx, sum_xa = lax.psum((local_xx, local_xa), ("gx", "gy"))
+
+    def _use_axis_part(x_part):
+        return jax.lax.psum(jax.lax.psum(x_part, "gy"), "gx")
+
+    sum_xx, sum_xa = _use_axis_part((local_xx, local_xa))
     return sum_xa * scale / (sum_xx * scale + 1e-06)
 
 

time: 180 us -> 162 us (0.900)
  blocking collectives: 88.1 us -> 73.1 us
  waiting for transfers between devices: 16.5 us -> 14.7 us
    psum x1 -> x2, blocking collectives: 44.4 us -> 29.3 us  [_use_axis_part(): return jax.lax.psum(jax.lax.psum(x_part, 'gy'), 'gx')]
  transfers between devices with their start and end apart: 19 -> 19, of which waited for: 6 -> 6; matrix products, arithmetic and copies ran while one was open for 5% -> 6% of each run, Pallas kernels for 0% -> 0%
where the time goes in v1:
time: 162 us; the launch traced here: 161 us
  blocking collectives  73.1 us (45%)
  starting transfers between devices  45.4 us (28%)
  waiting for transfers between devices  14.7 us (9%)
  other arithmetic  14 us (9%)
  local copies, waits for them, and re-layouts  7.16 us (4%)
  matrix products  5.21 us (3%)
    psum x1, blocking collectives, per_device(): gram_total, stiff_total = lax.psum((local_gram, local_stiff), ('gx', 'gy'))  43.8 us
    ppermute x9, starting transfers between devices, extended(): lax.ppermute(tail, axis, [(i, (i + 1) % count) for i in range(ends)])  32.4 us
    psum x2, blocking collectives, _use_axis_part(): return jax.lax.psum(jax.lax.psum(x_part, 'gy'), 'gx')  29.3 us
    ppermute x9, waiting for transfers between devices, extended(): lax.ppermute(head, axis, [((i + 1) % count, i) for i in range(ends)])  12.2 us
    ppermute x9, starting transfers between devices, extended(): lax.ppermute(head, axis, [((i + 1) % count, i) for i in range(ends)])  11.6 us
    concatenate x7, other arithmetic, extended(): jnp.concatenate([lax.ppermute(tail, axis, [(i, (i + 1) % count) for i in...  4.35 us
  transfers between devices with their start and end apart: 19, of which 6 were waited for; matrix products, arithmetic and copies ran while one was open for 6% of the time, Pallas kernels for 0%

profile of v1, /device:TPU:0, one launch (start us, length us, event | category | flops | bytes accessed | tf_op | source)
XLA Modules:
  0.0 161.0 jit_solution(4566177550763627244)
XLA Ops:
  0.6 0.9 convolution_bitcast_fusion.2
  1.6 1.1 broadcast_multiply_fusion
  2.7 0.7 pad_maximum_fusion.38
  3.5 2.4 %collective-permute-start = (f32[15,1,8,128]{3,2,1,0:T(8,128)S(1)}, f32[15,1,8,128]{3,2,1,0:T(8,128)S(1)}, u32[]{:S(2)}, u32[]{:S(2)}) collective-permute-start(f32[15,1,8,128]{3,2,1,0:T(8,128)S(1)} %get-tuple-element.51), channel_id=1, source_target_pairs={{0,8},{8,16},{16,24},{1,9},{9,17},{17,25},{2,10},{10,18},{18,26},{... | collective-permute-start | bytes 184328 | tf_op jit(solution)/shard_map/ppermute | solution.py:21
  5.8 1.3 collective-permute-start.1
  7.5 5.2 %collective-permute-start.5 = (f32[16,1,8,128]{3,0,2,1:T(8,128)S(1)}, f32[16,1,8,128]{3,0,2,1:T(8,128)S(1)}, u32[]{:S(2)}, u32[]{:S(2)}) collective-permute-start(f32[16,1,8,128]{3,0,2,1:T(8,128)S(1)} %get-tuple-element.50), channel_id=1, source_target_pairs={{0,8},{8,16},{16,24},{1,9},{9,17},{17,25},{2,10},{10,18},{18,26},{... | collective-permute-start | bytes 196616 | tf_op jit(solution)/shard_map/ppermute | solution.py:21
  12.6 1.3 collective-permute-start.4
  14.3 3.4 %collective-permute-start.2 = (f32[15,10,1,128]{3,0,2,1:T(8,128)S(1)}, f32[15,10,1,128]{3,0,2,1:T(8,128)S(1)}, u32[]{:S(2)}, u32[]{:S(2)}) collective-permute-start(f32[15,10,1,128]{3,0,2,1:T(8,128)S(1)} %copy.35), channel_id=1, source_target_pairs={{0,1},{1,2},{2,3},{3,4},{4,5},{5,6},{6,7},{8,9},{9,10},{10,11},{11... | collective-permute-start | bytes 230408 | tf_op jit(solution)/shard_map/ppermute | solution.py:21
  17.7 1.3 collective-permute-start.3
  19.4 1.3 collective-permute-start.6
  20.7 5.2 %collective-permute-start.7 = (f32[16,10,1,128]{3,0,2,1:T(8,128)S(1)}, f32[16,10,1,128]{3,0,2,1:T(8,128)S(1)}, u32[]{:S(2)}, u32[]{:S(2)}) collective-permute-start(f32[16,10,1,128]{3,0,2,1:T(8,128)S(1)} %get-tuple-element.39), channel_id=1, source_target_pairs={{0,1},{1,2},{2,3},{3,4},{4,5},{5,6},{6,7},{8,9},{9,10},{10,11},{11... | collective-permute-start | bytes 245768 | tf_op jit(solution)/shard_map/ppermute | solution.py:21
  26.1 2.8 %select_maximum_fusion = f32[15,10,10,130]{3,2,1,0:T(8,128)S(1)} fusion(f32[15,10,1,128]{3,2,1,0:T(1,128)S(1)} %copy.38, f32[15,10,1,128]{3,2,1,0:T(1,128)S(1)} %copy.37, f32[15,1,8,128]{3,2,1,0:T(8,128)S(1)} %collective-permute-done.1, f32[15,1,8,128]{3,2,1,0:T(8,128)S(1)} %collective-permute-done, f32[13,8,8,128]{3,2,1,0:T(8,128)S(1)} %broadcast_multiply_fusion, ...), kind=kLoop, calls=%fused_computation.13 | loop fusion | flops 3120000 | bytes 1548000 | tf_op jit(solution)/shard_map/concatenate | solution.py:19
  28.9 1.0 slice_bitcast_fusion.14
  30.6 0.8 multiply_reduce_fusion.1
  31.4 22.2 %all-reduce.6 = (f32[16]{0:T(128)S(1)}, f32[16]{0:T(128)S(1)}) all-reduce(f32[16]{0:T(128)S(1)} %multiply_reduce_fusion, f32[16]{0:T(128)S(1)} %get-tuple-element.18), channel_id=1, replica_groups=mesh['gx'=4,'gy'=8] {'gy'}, use_global_device_ids=true, to_apply=%region_4.5 | all-reduce | flops 32 | bytes 256 | tf_op jit(solution)/shard_map/psum | solution.py:82
  53.6 7.1 %all-reduce.7 = (f32[16]{0:T(128)S(1)}, f32[16]{0:T(128)S(1)}) all-reduce(f32[16]{0:T(128)S(1)} %get-tuple-element.14, f32[16]{0:T(128)S(1)} %get-tuple-element.15), channel_id=1, replica_groups=mesh['gx'=4,'gy'=8] {'gx'}, use_global_device_ids=true, to_apply=%region_5.6 | all-reduce | flops 32 | bytes 256 | tf_op jit(solution)/shard_map/psum | solution.py:82
  61.1 2.3 %collective-permute-start.8 = (f32[16,1,8,128]{3,0,2,1:T(8,128)S(1)}, f32[16,1,8,128]{3,0,2,1:T(8,128)S(1)}, u32[]{:S(2)}, u32[]{:S(2)}) collective-permute-start(f32[16,1,8,128]{3,0,2,1:T(8,128)S(1)} %get-tuple-element.47), channel_id=1, source_target_pairs={{0,8},{8,16},{16,24},{1,9},{9,17},{17,25},{2,10},{10,18},{18,26},{... | collective-permute-start | bytes 196616 | tf_op jit(solution)/shard_map/ppermute | solution.py:21
  63.4 1.3 collective-permute-start.9
  64.7 3.3 %collective-permute-done.9 = f32[16,1,8,128]{3,0,2,1:T(8,128)S(1)} collective-permute-done((f32[16,1,8,128]{3,0,2,1:T(8,128)S(1)}, f32[16,1,8,128]{3,0,2,1:T(8,128)S(1)}, u32[]{:S(2)}, u32[]{:S(2)}) %collective-permute-start.9) | collective-permute-done | bytes 65568 | tf_op jit(solution)/shard_map/ppermute | solution.py:23
  68.0 1.3 collective-permute-start.10
  69.4 1.3 collective-permute-start.11
  70.7 0.7 collective-permute-done.10
  71.4 4.3 %collective-permute-done.11 = f32[16,10,1,128]{3,0,2,1:T(8,128)S(1)} collective-permute-done((f32[16,10,1,128]{3,0,2,1:T(8,128)S(1)}, f32[16,10,1,128]{3,0,2,1:T(8,128)S(1)}, u32[]{:S(2)}, u32[]{:S(2)}) %collective-permute-start.11) | collective-permute-done | bytes 81952 | tf_op jit(solution)/shard_map/ppermute | solution.py:23
  76.2 0.8 fusion.53
  77.0 3.6 %collective-permute-start.12 = (f32[16,8,1,128]{3,0,2,1:T(8,128)S(1)}, f32[16,8,1,128]{3,0,2,1:T(8,128)S(1)}, u32[]{:S(2)}, u32[]{:S(2)}) collective-permute-start(f32[16,8,1,128]{3,0,2,1:T(8,128)S(1)} %get-tuple-element.45), channel_id=1, source_target_pairs={{0,1},{1,2},{2,3},{3,4},{4,5},{5,6},{6,7},{8,9},{9,10},{10,11},{11... | collective-permute-start | bytes 196616 | tf_op jit(solution)/shard_map/ppermute | solution.py:21
  80.6 1.3 collective-permute-start.13
  81.9 0.7 collective-permute-done.12
  82.6 4.6 %collective-permute-done.13 = f32[16,8,1,128]{3,0,2,1:T(8,128)S(1)} collective-permute-done((f32[16,8,1,128]{3,0,2,1:T(8,128)S(1)}, f32[16,8,1,128]{3,0,2,1:T(8,128)S(1)}, u32[]{:S(2)}, u32[]{:S(2)}) %collective-permute-start.13) | collective-permute-done | bytes 65568 | tf_op jit(solution)/shard_map/ppermute | solution.py:23
  87.3 1.3 collective-permute-start.14
  88.6 1.0 slice.508
  89.5 1.0 slice.550
  92.0 1.3 fusion.16
  93.4 1.3 collective-permute-start.15
  94.7 4.5 %collective-permute-start.16 = (f32[16,1,8,128]{3,0,2,1:T(8,128)S(1)}, f32[16,1,8,128]{3,0,2,1:T(8,128)S(1)}, u32[]{:S(2)}, u32[]{:S(2)}) collective-permute-start(f32[16,1,8,128]{3,0,2,1:T(8,128)S(1)} %get-tuple-element.43), channel_id=1, source_target_pairs={{0,8},{8,16},{16,24},{1,9},{9,17},{17,25},{2,10},{10,18},{18,26},{... | collective-permute-start | bytes 196616 | tf_op jit(solution)/shard_map/ppermute | solution.py:21
  99.2 1.0 copy.56
  100.1 1.3 collective-permute-start.17
  101.5 4.7 %collective-permute-start.18 = (f32[16,10,1,128]{3,0,2,1:T(8,128)S(1)}, f32[16,10,1,128]{3,0,2,1:T(8,128)S(1)}, u32[]{:S(2)}, u32[]{:S(2)}) collective-permute-start(f32[16,10,1,128]{3,0,2,1:T(8,128)S(1)} %get-tuple-element.35), channel_id=1, source_target_pairs={{0,1},{1,2},{2,3},{3,4},{4,5},{5,6},{6,7},{8,9},{9,10},{10,11},{11... | collective-permute-start | bytes 245768 | tf_op jit(solution)/shard_map/ppermute | solution.py:21
  106.2 1.0 convolution_bitcast_fusion.1
  107.2 1.0 collective-permute-done.18
  108.8 1.4 convolution_bitcast_fusion
  110.1 43.8 %all-reduce.5 = (f32[16,16]{1,0:T(8,128)S(1)}, f32[16,16]{1,0:T(8,128)S(1)}) all-reduce(f32[16,16]{1,0:T(8,128)S(1)} %convolution_bitcast_fusion.1, f32[16,16]{1,0:T(8,128)S(1)} %convolution_bitcast_fusion), channel_id=1, replica_groups=mesh['gx'=4,'gy'=8] {'gx','gy'}, use_global_device_ids=true, to_apply=%region_6.7 | all-reduce | flops 512 | bytes 4096 | tf_op jit(solution)/shard_map/psum | solution.py:128
  154.0 1.5 cholesky.17
  155.5 0.6 compare_reduce_fusion
  156.2 0.6 fusion.97
  156.8 1.2 custom-call.7
  158.2 0.9 fusion.98
  159.3 0.7 fusion.118
  160.0 1.0 copy.55
  (97 shorter events, 5.2 us)
Async XLA Ops:
  0.6 6.5 %copy-start = (f32[16,8,8,128]{3,2,1,0:T(8,128)S(1)}, f32[16,8,8,128]{3,2,1,0:T(8,128)}, u32[]{:S(2)}) copy-start(f32[16,8,8,128]{3,2,1,0:T(8,128)} %param.8) | copy-start | bytes 1572868
  1.6 12.6 %copy-start.1 = (f32[8,8,128]{2,1,0:T(8,128)S(1)}, f32[8,8,128]{2,1,0:T(8,128)}, u32[]{:S(2)}) copy-start(f32[8,8,128]{2,1,0:T(8,128)} %param.11) | copy-start | bytes 98308
  1.6 12.6 %copy-start.3 = (f32[8,8,128]{2,1,0:T(8,128)S(1)}, f32[8,8,128]{2,1,0:T(8,128)}, u32[]{:S(2)}) copy-start(f32[8,8,128]{2,1,0:T(8,128)} %param.10) | copy-start | bytes 98308
  3.5 10.7 %collective-permute-start = (f32[15,1,8,128]{3,2,1,0:T(8,128)S(1)}, f32[15,1,8,128]{3,2,1,0:T(8,128)S(1)}, u32[]{:S(2)}, u32[]{:S(2)}) collective-permute-start(f32[15,1,8,128]{3,2,1,0:T(8,128)S(1)} %get-tuple-element.51), channel_id=1, source_target_pairs={{0,8},{8,16},{16,24},{1,9},{9,17},{17,25},{2,10},{10,18},{18,26},{... | collective-permute-start | bytes 184328 | tf_op jit(solution)/shard_map/ppermute | solution.py:21
  5.8 8.3 %collective-permute-start.1 = (f32[15,1,8,128]{3,2,1,0:T(8,128)S(1)}, f32[15,1,8,128]{3,2,1,0:T(8,128)S(1)}, u32[]{:S(2)}, u32[]{:S(2)}) collective-permute-start(f32[15,1,8,128]{3,2,1,0:T(8,128)S(1)} %get-tuple-element.52), channel_id=1, source_target_pairs={{8,0},{16,8},{24,16},{9,1},{17,9},{25,17},{10,2},{18,10},{26,18},{... | collective-permute-start | bytes 184328 | tf_op jit(solution)/shard_map/ppermute | solution.py:23
  7.5 11.6 %collective-permute-start.5 = (f32[16,1,8,128]{3,0,2,1:T(8,128)S(1)}, f32[16,1,8,128]{3,0,2,1:T(8,128)S(1)}, u32[]{:S(2)}, u32[]{:S(2)}) collective-permute-start(f32[16,1,8,128]{3,0,2,1:T(8,128)S(1)} %get-tuple-element.50), channel_id=1, source_target_pairs={{0,8},{8,16},{16,24},{1,9},{9,17},{17,25},{2,10},{10,18},{18,26},{... | collective-permute-start | bytes 196616 | tf_op jit(solution)/shard_map/ppermute | solution.py:21
  12.6 6.7 %collective-permute-start.4 = (f32[16,1,8,128]{3,0,2,1:T(8,128)S(1)}, f32[16,1,8,128]{3,0,2,1:T(8,128)S(1)}, u32[]{:S(2)}, u32[]{:S(2)}) collective-permute-start(f32[16,1,8,128]{3,0,2,1:T(8,128)S(1)} %get-tuple-element.49), channel_id=1, source_target_pairs={{8,0},{16,8},{24,16},{9,1},{17,9},{25,17},{10,2},{18,10},{26,18},{... | collective-permute-start | bytes 196616 | tf_op jit(solution)/shard_map/ppermute | solution.py:23
  14.3 11.6 %collective-permute-start.2 = (f32[15,10,1,128]{3,0,2,1:T(8,128)S(1)}, f32[15,10,1,128]{3,0,2,1:T(8,128)S(1)}, u32[]{:S(2)}, u32[]{:S(2)}) collective-permute-start(f32[15,10,1,128]{3,0,2,1:T(8,128)S(1)} %copy.35), channel_id=1, source_target_pairs={{0,1},{1,2},{2,3},{3,4},{4,5},{5,6},{6,7},{8,9},{9,10},{10,11},{11... | collective-permute-start | bytes 230408 | tf_op jit(solution)/shard_map/ppermute | solution.py:21
  17.7 8.3 %collective-permute-start.3 = (f32[15,10,1,128]{3,0,2,1:T(8,128)S(1)}, f32[15,10,1,128]{3,0,2,1:T(8,128)S(1)}, u32[]{:S(2)}, u32[]{:S(2)}) collective-permute-start(f32[15,10,1,128]{3,0,2,1:T(8,128)S(1)} %copy.36), channel_id=1, source_target_pairs={{1,0},{2,1},{3,2},{4,3},{5,4},{6,5},{7,6},{9,8},{10,9},{11,10},{12... | collective-permute-start | bytes 230408 | tf_op jit(solution)/shard_map/ppermute | solution.py:23
  19.4 10.7 %collective-permute-start.6 = (f32[16,10,1,128]{3,0,2,1:T(8,128)S(1)}, f32[16,10,1,128]{3,0,2,1:T(8,128)S(1)}, u32[]{:S(2)}, u32[]{:S(2)}) collective-permute-start(f32[16,10,1,128]{3,0,2,1:T(8,128)S(1)} %get-tuple-element.40), channel_id=1, source_target_pairs={{1,0},{2,1},{3,2},{4,3},{5,4},{6,5},{7,6},{9,8},{10,9},{11,10},{12... | collective-permute-start | bytes 245768 | tf_op jit(solution)/shard_map/ppermute | solution.py:23
  20.7 9.4 %collective-permute-start.7 = (f32[16,10,1,128]{3,0,2,1:T(8,128)S(1)}, f32[16,10,1,128]{3,0,2,1:T(8,128)S(1)}, u32[]{:S(2)}, u32[]{:S(2)}) collective-permute-start(f32[16,10,1,128]{3,0,2,1:T(8,128)S(1)} %get-tuple-element.39), channel_id=1, source_target_pairs={{0,1},{1,2},{2,3},{3,4},{4,5},{5,6},{6,7},{8,9},{9,10},{10,11},{11... | collective-permute-start | bytes 245768 | tf_op jit(solution)/shard_map/ppermute | solution.py:21
  30.0 1.4 copy-start.4
  30.0 1.3 copy-start.6
  30.1 1.3 copy-start.8
  30.1 1.3 copy-start.10
  30.1 1.3 copy-start.12
  30.1 1.3 copy-start.14
  61.1 3.6 %collective-permute-start.8 = (f32[16,1,8,128]{3,0,2,1:T(8,128)S(1)}, f32[16,1,8,128]{3,0,2,1:T(8,128)S(1)}, u32[]{:S(2)}, u32[]{:S(2)}) collective-permute-start(f32[16,1,8,128]{3,0,2,1:T(8,128)S(1)} %get-tuple-element.47), channel_id=1, source_target_pairs={{0,8},{8,16},{16,24},{1,9},{9,17},{17,25},{2,10},{10,18},{18,26},{... | collective-permute-start | bytes 196616 | tf_op jit(solution)/shard_map/ppermute | solution.py:21
  63.4 4.6 %collective-permute-start.9 = (f32[16,1,8,128]{3,0,2,1:T(8,128)S(1)}, f32[16,1,8,128]{3,0,2,1:T(8,128)S(1)}, u32[]{:S(2)}, u32[]{:S(2)}) collective-permute-start(f32[16,1,8,128]{3,0,2,1:T(8,128)S(1)} %get-tuple-element.48), channel_id=1, source_target_pairs={{8,0},{16,8},{24,16},{9,1},{17,9},{25,17},{10,2},{18,10},{26,18},{... | collective-permute-start | bytes 196616 | tf_op jit(solution)/shard_map/ppermute | solution.py:23
  68.0 3.3 %collective-permute-start.10 = (f32[16,10,1,128]{3,0,2,1:T(8,128)S(1)}, f32[16,10,1,128]{3,0,2,1:T(8,128)S(1)}, u32[]{:S(2)}, u32[]{:S(2)}) collective-permute-start(f32[16,10,1,128]{3,0,2,1:T(8,128)S(1)} %get-tuple-element.37), channel_id=1, source_target_pairs={{0,1},{1,2},{2,3},{3,4},{4,5},{5,6},{6,7},{8,9},{9,10},{10,11},{11... | collective-permute-start | bytes 245768 | tf_op jit(solution)/shard_map/ppermute | solution.py:21
  69.4 6.3 %collective-permute-start.11 = (f32[16,10,1,128]{3,0,2,1:T(8,128)S(1)}, f32[16,10,1,128]{3,0,2,1:T(8,128)S(1)}, u32[]{:S(2)}, u32[]{:S(2)}) collective-permute-start(f32[16,10,1,128]{3,0,2,1:T(8,128)S(1)} %get-tuple-element.38), channel_id=1, source_target_pairs={{1,0},{2,1},{3,2},{4,3},{5,4},{6,5},{7,6},{9,8},{10,9},{11,10},{12... | collective-permute-start | bytes 245768 | tf_op jit(solution)/shard_map/ppermute | solution.py:23
  77.0 5.6 %collective-permute-start.12 = (f32[16,8,1,128]{3,0,2,1:T(8,128)S(1)}, f32[16,8,1,128]{3,0,2,1:T(8,128)S(1)}, u32[]{:S(2)}, u32[]{:S(2)}) collective-permute-start(f32[16,8,1,128]{3,0,2,1:T(8,128)S(1)} %get-tuple-element.45), channel_id=1, source_target_pairs={{0,1},{1,2},{2,3},{3,4},{4,5},{5,6},{6,7},{8,9},{9,10},{10,11},{11... | collective-permute-start | bytes 196616 | tf_op jit(solution)/shard_map/ppermute | solution.py:21
  80.6 6.6 %collective-permute-start.13 = (f32[16,8,1,128]{3,0,2,1:T(8,128)S(1)}, f32[16,8,1,128]{3,0,2,1:T(8,128)S(1)}, u32[]{:S(2)}, u32[]{:S(2)}) collective-permute-start(f32[16,8,1,128]{3,0,2,1:T(8,128)S(1)} %get-tuple-element.46), channel_id=1, source_target_pairs={{1,0},{2,1},{3,2},{4,3},{5,4},{6,5},{7,6},{9,8},{10,9},{11,10},{12... | collective-permute-start | bytes 196616 | tf_op jit(solution)/shard_map/ppermute | solution.py:23
  87.3 4.0 %collective-permute-start.14 = (f32[16,1,10,128]{3,0,2,1:T(8,128)S(1)}, f32[16,1,10,128]{3,0,2,1:T(8,128)S(1)}, u32[]{:S(2)}, u32[]{:S(2)}) collective-permute-start(f32[16,1,10,128]{3,0,2,1:T(8,128)S(1)} %pad_maximum_fusion.26), channel_id=1, source_target_pairs={{8,0},{16,8},{24,16},{9,1},{17,9},{25,17},{10,2},{18,10},{26,18},{... | collective-permute-start | bytes 245768 | tf_op jit(solution)/shard_map/ppermute | solution.py:33
  91.0 1.0 copy-start.2
  91.0 1.0 copy-start.17
  93.3 12.8 %copy-start.16 = (f32[16]{0:T(128)S(1)}, f32[16]{0:T(128)}, u32[]{:S(2)}) copy-start(f32[16]{0:T(128)} %param.14) | copy-start | bytes 196
  93.4 6.7 %collective-permute-start.15 = (f32[16,1,8,128]{3,0,2,1:T(8,128)S(1)}, f32[16,1,8,128]{3,0,2,1:T(8,128)S(1)}, u32[]{:S(2)}, u32[]{:S(2)}) collective-permute-start(f32[16,1,8,128]{3,0,2,1:T(8,128)S(1)} %get-tuple-element.44), channel_id=1, source_target_pairs={{8,0},{16,8},{24,16},{9,1},{17,9},{25,17},{10,2},{18,10},{26,18},{... | collective-permute-start | bytes 196616 | tf_op jit(solution)/shard_map/ppermute | solution.py:23
  94.7 5.4 %collective-permute-start.16 = (f32[16,1,8,128]{3,0,2,1:T(8,128)S(1)}, f32[16,1,8,128]{3,0,2,1:T(8,128)S(1)}, u32[]{:S(2)}, u32[]{:S(2)}) collective-permute-start(f32[16,1,8,128]{3,0,2,1:T(8,128)S(1)} %get-tuple-element.43), channel_id=1, source_target_pairs={{0,8},{8,16},{16,24},{1,9},{9,17},{17,25},{2,10},{10,18},{18,26},{... | collective-permute-start | bytes 196616 | tf_op jit(solution)/shard_map/ppermute | solution.py:21
  100.1 7.0 %collective-permute-start.17 = (f32[16,10,1,128]{3,0,2,1:T(8,128)S(1)}, f32[16,10,1,128]{3,0,2,1:T(8,128)S(1)}, u32[]{:S(2)}, u32[]{:S(2)}) collective-permute-start(f32[16,10,1,128]{3,0,2,1:T(8,128)S(1)} %get-tuple-element.36), channel_id=1, source_target_pairs={{1,0},{2,1},{3,2},{4,3},{5,4},{6,5},{7,6},{9,8},{10,9},{11,10},{12... | collective-permute-start | bytes 245768 | tf_op jit(solution)/shard_map/ppermute | solution.py:23
  101.4 7.3 %copy-start.5 = (f32[8,8,128]{2,1,0:T(8,128)S(1)}, f32[8,8,128]{2,1,0:T(8,128)}, u32[]{:S(2)}) copy-start(f32[8,8,128]{2,1,0:T(8,128)} %copy-done.4) | copy-start | bytes 98308
  101.4 7.3 %copy-start.7 = (f32[8,8,128]{2,1,0:T(8,128)S(1)}, f32[8,8,128]{2,1,0:T(8,128)}, u32[]{:S(2)}) copy-start(f32[8,8,128]{2,1,0:T(8,128)} %copy-done.6) | copy-start | bytes 98308
  101.5 7.3 %copy-start.9 = (f32[8,8,128]{2,1,0:T(8,128)S(1)}, f32[8,8,128]{2,1,0:T(8,128)}, u32[]{:S(2)}) copy-start(f32[8,8,128]{2,1,0:T(8,128)} %copy-done.8) | copy-start | bytes 98308
  101.5 7.3 %copy-start.11 = (f32[8,8,128]{2,1,0:T(8,128)S(1)}, f32[8,8,128]{2,1,0:T(8,128)}, u32[]{:S(2)}) copy-start(f32[8,8,128]{2,1,0:T(8,128)} %copy-done.10) | copy-start | bytes 98308
  101.5 7.3 %copy-start.13 = (f32[8,8,128]{2,1,0:T(8,128)S(1)}, f32[8,8,128]{2,1,0:T(8,128)}, u32[]{:S(2)}) copy-start(f32[8,8,128]{2,1,0:T(8,128)} %copy-done.12) | copy-start | bytes 98308
  101.5 7.3 %copy-start.15 = (f32[8,8,128]{2,1,0:T(8,128)S(1)}, f32[8,8,128]{2,1,0:T(8,128)}, u32[]{:S(2)}) copy-start(f32[8,8,128]{2,1,0:T(8,128)} %copy-done.14) | copy-start | bytes 98308
  101.5 6.7 %collective-permute-start.18 = (f32[16,10,1,128]{3,0,2,1:T(8,128)S(1)}, f32[16,10,1,128]{3,0,2,1:T(8,128)S(1)}, u32[]{:S(2)}, u32[]{:S(2)}) collective-permute-start(f32[16,10,1,128]{3,0,2,1:T(8,128)S(1)} %get-tuple-element.35), channel_id=1, source_target_pairs={{0,1},{1,2},{2,3},{3,4},{4,5},{5,6},{6,7},{8,9},{9,10},{10,11},{11... | collective-permute-start | bytes 245768 | tf_op jit(solution)/shard_map/ppermute | solution.py:21
